TPU v7x, 128 devices: a whole 4x4x4 slice. The times are simulated.
128 devices in a mesh: space: 32 (over z, x, core), head: 4 (over y).
Axes of the slice: x: 4, y: 4, z: 4, core: 2. Of those that a mesh axis runs over, the one named last changes fastest.
Arguments:
- tokens: bfloat16 [32768, 1024], P('space'), may hold values from -70 to 70
- w_qkv: bfloat16 [1024, 3, 1024], P(None, None, 'head'), may hold values from -7 to 7
- w_out: bfloat16 [1024, 1024], P('head'), may hold values from -0.5 to 0.5
- neighbours: int32 [256, 9], P('space'), may hold values from 0 to 71, as said below
- requests: int32 [32, 32, 2], P('space'), may hold values from -1 to 7, as said below
- cotangent: bfloat16 [32768, 1024], P('space', 'head'), may hold values from -6 to 6
Outputs:
- layer_out: bfloat16 [32768, 1024], P('space', 'head')
- grad_tokens: bfloat16 [32768, 1024], P('space', 'head')
- grad_w_qkv: float32 [1024, 3, 1024], P('space', None, 'head')
- grad_w_out: float32 [1024, 1024], P('head', 'space')
Inputs may be any that keep to these rules, and one draw needn't show every extreme that they name: `neighbours`: row t starts with t % 8 itself, then 3 other tiles of the same device, then 5 slot entries 8 + p * 2 + c; every slot entry names a filled request of that device, every filled request is named by some tile of that device, and no row names a tile twice. requests[d, p, c] is a tile of device p by its index within p, or -1 for an empty slot; filled slots come first and are distinct, requests[d, d] is empty, and in every draw some device fills all 2 slots towards some other device.
All inputs are finite; a program needn't handle non-finite values.
Results may differ from a plain program's by a relative error of at most 0.02.
The roundings to bfloat16 on the way count: a program that leaves them out, or rounds other values in their place, can miss the bound.
Values may be sent and summed in bfloat16 or wider, within the bound.
A program may use at most 192 MiB of HBM per device.

v0:
```python
import functools

import jax
import jax.numpy as jnp
from jax import lax
from jax.experimental import pallas as pl
from jax.experimental.pallas import tpu as pltpu
from jax.sharding import PartitionSpec as P

HEAD_DIM = 64
NEIGHBOURS = 9
NEAR = 4
REACHES = (1,)
AT_ONCE = 2
CORE_VMEM = 62 * 2**20
SLOTS = 2
EPSILON = 1e-05
F32 = jnp.float32
BF16 = jnp.bfloat16
VMEM_BYTES = 60 * 2**20


def dot(a, b, dims):
    return lax.dot_general(a, b, (dims, ((), ())), preferred_element_type=F32)


def norm_rows(tokens):
    values = tokens.astype(F32)
    mean = jnp.mean(values, axis=1, keepdims=True)
    centred = values - mean
    inverse = lax.rsqrt(jnp.mean(centred * centred, axis=1, keepdims=True) + EPSILON)
    return centred * inverse, mean, inverse


def head_cut(h):
    return slice(h * HEAD_DIM, (h + 1) * HEAD_DIM)


def project_kernel(peers, groups, tokens_ref, w_ref, requests_ref, normed_ref, q_ref, kv_ref, stats_ref, table_ref, sems, own_sem):
    me = lax.axis_index("space")
    step = pl.program_id(0)
    heads = kv_ref.shape[1]
    own = pltpu.make_async_copy(requests_ref, table_ref.at[me], own_sem)

    def along(r, peer):
        return copy_to(requests_ref, table_ref.at[me], sems, r, {"space": peer})

    @pl.when(step == 0)
    def _():
        own.start()
        signal_all(peers, groups)

    standard, mean, inverse = norm_rows(tokens_ref[...])
    normed = standard.astype(BF16)
    normed_ref[...] = normed
    stats_ref[...] = jnp.concatenate([mean, inverse], 1).T
    q = dot(normed, w_ref[0], ((1,), (0,))).astype(BF16)
    q_ref[...] = (q.astype(F32) * HEAD_DIM ** (-0.5)).astype(BF16)
    k = dot(normed, w_ref[1], ((1,), (0,))).astype(BF16)
    v = dot(normed, w_ref[2], ((1,), (0,))).astype(BF16)
    for h in range(heads):
        pair = jnp.concatenate([k[:, head_cut(h)], v[:, head_cut(h)]], 1)
        kv_ref[:, h] = pair.reshape(kv_ref.shape[0], kv_ref.shape[2], 2 * HEAD_DIM)

    @pl.when(step == 2)
    def _():
        pl.semaphore_wait(pltpu.get_barrier_semaphore(), peers + groups - 2)

        @pl.loop(1, peers)
        def _(r):
            along(r, lax.rem(me + r, peers)).start()

    @pl.when(step == pl.num_programs(0) - 1)
    def _():
        @pl.loop(1, peers)
        def _(r):
            along(r, lax.rem(me + r, peers)).wait()

        own.wait()


def project(tokens, w3, requests, tile_rows, peers, groups, number):
    rows, width = tokens.shape
    cols = w3.shape[2]
    step = 256
    kv_block = (step // tile_rows, cols // HEAD_DIM, tile_rows, 2 * HEAD_DIM)
    return pl.pallas_call(
        functools.partial(project_kernel, peers, groups),
        grid=(rows // step,),
        in_specs=[
            pl.BlockSpec((step, width), lambda i: (i, 0)),
            pl.BlockSpec((3, width, cols), lambda i: (0, 0, 0)),
            pl.BlockSpec(memory_space=pl.ANY),
        ],
        out_specs=[
            pl.BlockSpec((step, width), lambda i: (i, 0)),
            pl.BlockSpec((step, cols), lambda i: (i, 0)),
            pl.BlockSpec(kv_block, lambda i: (i, 0, 0, 0)),
            pl.BlockSpec((2, step), lambda i: (0, i)),
            pl.BlockSpec(memory_space=pl.ANY),
        ],
        out_shape=[
            jax.ShapeDtypeStruct((rows, width), BF16),
            jax.ShapeDtypeStruct((rows, cols), BF16),
            jax.ShapeDtypeStruct((rows // tile_rows,) + kv_block[1:], BF16),
            jax.ShapeDtypeStruct((2, rows), F32),
            jax.ShapeDtypeStruct((peers,) + requests.shape, requests.dtype),
        ],
        scratch_shapes=[pltpu.SemaphoreType.DMA((2, peers)), pltpu.SemaphoreType.DMA],
        compiler_params=pltpu.CompilerParams(
            collective_id=number, has_side_effects=True, vmem_limit_bytes=VMEM_BYTES
        ),
    )(tokens, w3, requests)


def copy_to(src, dst, sems, index, device):
    return pltpu.make_async_remote_copy(
        src_ref=src,
        dst_ref=dst,
        send_sem=sems.at[0, index],
        recv_sem=sems.at[1, index],
        device_id=device,
        device_id_type=pl.DeviceIdType.MESH,
    )


def greet(peers, groups):
    signal_all(peers, groups)
    pl.semaphore_wait(pltpu.get_barrier_semaphore(), peers + groups - 2)


def signal_all(peers, groups):
    barrier = pltpu.get_barrier_semaphore()
    me, group = lax.axis_index("space"), lax.axis_index("head")

    @pl.loop(1, peers)
    def _(r):
        pl.semaphore_signal(
            barrier,
            inc=1,
            device_id={"space": lax.rem(me + r, peers)},
            device_id_type=pl.DeviceIdType.MESH,
        )

    for k in range(1, groups):
        pl.semaphore_signal(
            barrier,
            inc=1,
            device_id={"head": lax.rem(group + k, groups)},
            device_id_type=pl.DeviceIdType.MESH,
        )


def axis_steps(q):
    far = 1 + 2 * lax.rem(q, 2)
    return (q // 2) * far, (1 - q // 2) * far


def corner_steps(q):
    return 1 + 2 * lax.rem(q, 2), 1 + 2 * lax.rem(lax.rem(q, 2) + q // 2, 2)


def across_steps(q):
    return 2 * q, 2 - 2 * q


def knight_steps(q):
    odd = lax.rem(q, 2)
    return 2 * odd + (1 - odd) * (1 + q), 2 * (1 - odd) + odd * q


def opposite_steps(q):
    return 2 + 0 * q, 2 + 0 * q


GROUPS = (
    (4, axis_steps),
    (4, corner_steps),
    (2, across_steps),
    (4, knight_steps),
    (1, opposite_steps),
)


def each_peer(act):
    act(0, (0, 0, 1))
    base = 1
    for size, steps in GROUPS:

        @pl.loop(0, 2 * size)
        def _(n, size=size, steps=steps, base=base):
            act(base + n, (*steps(lax.rem(n, size)), n // size))

        base += 2 * size


def torus_peer(me, step):
    z = lax.rem(me // 8 + step[0], 4)
    x = lax.rem(lax.rem(me // 2, 4) + step[1], 4)
    return z * 8 + x * 2 + lax.rem(lax.rem(me, 2) + step[2], 2)


def torus_source(me, step):
    return torus_peer(me, (4 - step[0], 4 - step[1], step[2]))


def second_ranges(peers, reach):
    if 2 * reach >= peers - 1:
        return [(1, peers)]
    return [(1, reach + 1), (peers - reach, peers)]


def core_kernel(peers, groups, reach, wanted_ref, entries_ref, perm_ref, same_ref, last_ref, q_ref, kv_ref, w_out_ref, cot_ref, grad_kv_ref, dq_ref, early_ref, atts_ref, staged0, staged1, got0, got1, landed0, landed1, held, near_runs, far_runs, running, total, cots, grad_att, att, part, kv_sems, back_sems, row_sems, own_sems):
    me, group = lax.axis_index("space"), lax.axis_index("head")
    staged, got, landed = (staged0, staged1), (got0, got1), (landed0, landed1)
    tiles, heads, span = kv_ref.shape[:3]
    cols = q_ref.shape[1]
    share = cot_ref.shape[1]
    rows = q_ref.shape[0]
    half_heads = heads // 2
    near_count = tiles * NEAR
    entry_count = tiles * NEIGHBOURS
    greet(peers, groups)

    def across(kind, k):
        peer = lax.rem(group + k, groups)
        source = cot_ref if kind == 0 else part.at[peer]
        target = (cots, atts_ref)[kind].at[group]
        return copy_to(source, target, row_sems, kind * groups + k, {"head": peer})

    def send(half, c, r, peer):
        return copy_to(
            staged[half].at[c * peers + r],
            got[half].at[me * SLOTS + c],
            kv_sems.at[half],
            c * peers + r,
            {"space": peer},
        )

    def give(half, c, r, peer):
        return copy_to(
            staged[half].at[c * peers + r],
            landed[half].at[c * peers + r],
            back_sems.at[half],
            c * peers + r,
            {"space": peer},
        )

    own_cot = pltpu.make_async_copy(cot_ref, cots.at[group], own_sems.at[0])
    own_cot.start()
    for k in range(1, groups):
        across(0, k).start()
    for half in range(2):
        cut = slice(half * half_heads, (half + 1) * half_heads)

        @each_peer
        def _(i, step, half=half, cut=cut):
            peer = torus_peer(me, step)
            staged[half][i] = kv_ref[jnp.maximum(wanted_ref[peer], 0), cut]
            send(half, 0, i, peer).start()

        for low, high in second_ranges(peers, reach):

            @pl.loop(low, high)
            def _(r, half=half, cut=cut):
                peer = lax.rem(me + r, peers)
                tile = jnp.maximum(wanted_ref[peers + peer], 0)
                staged[half][peers + r] = kv_ref[tile, cut]
                send(half, 1, r, peer).start()

    for k in range(1, groups):
        across(0, k).wait()
    own_cot.wait()
    step_rows = 2 * span

    @pl.loop(0, rows // step_rows)
    def _(i):
        at = pl.ds(pl.multiple_of(i * step_rows, step_rows), step_rows)
        cot = jnp.concatenate([cots[g, at, :] for g in range(groups)], 1)
        grad_att[at, :] = dot(cot, w_out_ref[...], ((1,), (1,))).astype(BF16)

    left = lax.broadcasted_iota(jnp.int32, (128, 128), 1) < HEAD_DIM
    upper = lax.broadcasted_iota(jnp.int32, (128, 128), 0) < HEAD_DIM

    def attend(half):
        @pl.loop(0, tiles // AT_ONCE)
        def _(turn):
            def tile_rows(u):
                return pl.ds(pl.multiple_of((turn * AT_ONCE + u) * span, span), span)

            def begin(u, hh):
                h = half * half_heads + hh
                at = tile_rows(u)
                first = (turn * AT_ONCE + u) * NEIGHBOURS
                pair = jnp.concatenate([q_ref[at, head_cut(h)], grad_att[at, head_cut(h)]], 1)
                pair_t = pair.T
                zero = jnp.zeros_like(pair)
                stacked = jnp.concatenate(
                    [jnp.where(left, pair, zero), jnp.where(left, zero, pair)], 0
                )
                stacked_t = jnp.concatenate(
                    [jnp.where(upper, pair_t, zero), jnp.where(upper, zero, pair_t)], 1
                )
                keys = [kv_ref[entries_ref[first + j], h] for j in range(NEAR)]
                keys += [
                    got[half][jnp.maximum(entries_ref[first + j] - tiles, 0), hh]
                    for j in range(NEAR, NEIGHBOURS)
                ]
                kv = jnp.concatenate(keys, 0)
                return stacked_t, kv, dot(stacked, kv, ((1,), (1,)))

            mixed = {}
            order = [(u, hh) for u in range(AT_ONCE) for hh in range(half_heads)]
            following = begin(*order[0])
            for n, (u, hh) in enumerate(order):
                stacked_t, kv, both = following
                if n + 1 < len(order):
                    following = begin(*order[n + 1])
                scores = both[:128]
                grad_prob = both[128:]
                weights = jnp.exp(scores - jnp.max(scores, axis=1, keepdims=True))
                inverse = 1.0 / jnp.sum(weights, axis=1, keepdims=True)
                row_delta = jnp.sum(weights * grad_prob, axis=1, keepdims=True) * inverse
                likely = weights * inverse
                grad_score = likely * (grad_prob - row_delta)
                factors = jnp.concatenate([grad_score.astype(BF16), likely.astype(BF16)], 0)
                mixed[u, hh] = dot(factors, kv, ((1,), (0,)))
                grad_kv_t = dot(stacked_t, factors, ((1,), (0,)))
                first = (turn * AT_ONCE + u) * NEIGHBOURS
                for j in range(NEIGHBOURS):
                    held[first + j, hh] = grad_kv_t[:, j * 128 : (j + 1) * 128]
            lanes = slice(half * half_heads * HEAD_DIM, (half + 1) * half_heads * HEAD_DIM)
            for u in range(AT_ONCE):
                both = [mixed[u, hh] for hh in range(half_heads)]
                dq = jnp.concatenate([m[:128, :HEAD_DIM] for m in both], 1)
                dq_ref[tile_rows(u), lanes] = (dq * HEAD_DIM ** (-0.5)).astype(BF16)
                attended = jnp.concatenate([m[128:, HEAD_DIM:] for m in both], 1)
                att[tile_rows(u), lanes] = attended.astype(BF16)

        def run(i):
            keep = jnp.where(same_ref[i] > 0, 1.0, 0.0)
            value = running[...] * keep + held[perm_ref[i]]
            running[...] = value
            return value

        running[...] = jnp.zeros_like(running)

        @pl.loop(0, near_count)
        def _(i):
            near_runs[i] = run(i)

        @pl.loop(near_count, entry_count)
        def _(i):
            far_runs[i - near_count] = run(i).astype(BF16)

        @each_peer
        def _(i, step):
            peer = torus_peer(me, step)
            place = jnp.maximum(last_ref[tiles + peer * SLOTS] - near_count, 0)
            staged[half][i] = far_runs[place]
            give(half, 0, i, peer).start()

        for low, high in second_ranges(peers, reach):

            @pl.loop(low, high)
            def _(r):
                peer = lax.rem(me + r, peers)
                place = jnp.maximum(last_ref[tiles + peer * SLOTS + 1] - near_count, 0)
                staged[half][peers + r] = far_runs[place]
                give(half, 1, r, peer).start()

        @pl.loop(0, tiles)
        def _(t):
            total[half, t] = near_runs[jnp.maximum(last_ref[t], 0)]

    beside = lax.rem(me + 1, peers)
    for half in range(2):

        @pl.loop(0, (peers - 1))
        def _(i, half=half):
            send(half, 0, i, beside).wait()

        for low, high in second_ranges(peers, reach):

            @pl.loop(low, high)
            def _(r, half=half):
                send(half, 1, r, beside).wait()

        attend(half)

    own_att = pltpu.make_async_copy(part.at[group], atts_ref.at[group], own_sems.at[1])
    for g in range(groups):

        @pl.loop(0, rows // step_rows)
        def _(i, g=g):
            at = pl.ds(pl.multiple_of(i * step_rows, step_rows), step_rows)
            lanes = slice(g * share, (g + 1) * share)
            made = dot(att[at, :], w_out_ref[:, lanes], ((1,), (0,)))
            part[g, at, :] = made.astype(BF16)

    own_att.start()
    for k in range(1, groups):
        across(1, k).start()
    for g in range(groups):
        made = dot(cots[g], att[...], ((0,), (0,)))
        early_ref[g * share : (g + 1) * share, :] = made.astype(BF16)

    for half in range(2):

        def add(c, r, source, half=half):
            tile = wanted_ref[c * peers + source]
            block = landed[half][c * peers + r].astype(F32)

            @pl.loop(0, tiles)
            def _(t):
                total[half, t] += block * jnp.where(tile == t, 1.0, 0.0)

        @each_peer
        def _(i, step, half=half, add=add):
            give(half, 0, i, torus_peer(me, step)).wait()
            add(0, i, torus_source(me, step))

        for low, high in second_ranges(peers, reach):

            @pl.loop(low, high)
            def _(r, half=half, add=add):
                give(half, 1, r, lax.rem(me + r, peers)).wait()
                add(1, r, lax.rem(me + peers - r, peers))

        grad_kv_ref[:, half * half_heads : (half + 1) * half_heads] = total[half].astype(BF16)
    for k in range(1, groups):
        across(1, k).wait()
    own_att.wait()


def core(wanted, entries, perm, same, last, q, kv, w_out, cot, peers, groups, reach, number):
    tiles, heads, span, mixed = kv.shape
    rows, cols = q.shape
    width = w_out.shape[1]
    half = (heads // 2, span, mixed)
    slots = pltpu.VMEM((peers * SLOTS,) + half, BF16)
    smem = pl.BlockSpec(memory_space=pltpu.SMEM)
    vmem = pl.BlockSpec(memory_space=pltpu.VMEM)
    whole = pl.BlockSpec(memory_space=pl.ANY)
    parts = (groups,) + cot.shape
    return pl.pallas_call(
        functools.partial(core_kernel, peers, groups, reach),
        in_specs=[smem] * 5 + [vmem] * 3 + [whole],
        out_specs=[vmem] * 3 + [whole],
        out_shape=[
            jax.ShapeDtypeStruct(kv.shape, BF16),
            jax.ShapeDtypeStruct(q.shape, BF16),
            jax.ShapeDtypeStruct((width, cols), BF16),
            jax.ShapeDtypeStruct(parts, BF16),
        ],
        scratch_shapes=[slots] * 6
        + [
            pltpu.VMEM((tiles * NEIGHBOURS,) + half, F32),
            pltpu.VMEM((tiles * NEAR,) + half, F32),
            pltpu.VMEM((tiles * (NEIGHBOURS - NEAR),) + half, BF16),
            pltpu.VMEM(half, F32),
            pltpu.VMEM((2, tiles) + half, F32),
            pltpu.VMEM(parts, BF16),
            pltpu.VMEM(q.shape, BF16),
            pltpu.VMEM(q.shape, BF16),
            pltpu.VMEM(parts, BF16),
            pltpu.SemaphoreType.DMA((2, 2, SLOTS * peers)),
            pltpu.SemaphoreType.DMA((2, 2, SLOTS * peers)),
            pltpu.SemaphoreType.DMA((2, 2 * groups)),
            pltpu.SemaphoreType.DMA((2,)),
        ],
        compiler_params=pltpu.CompilerParams(
            collective_id=number, has_side_effects=True, vmem_limit_bytes=CORE_VMEM
        ),
    )(wanted, entries, perm, same, last, q, kv, w_out, cot)


def finish_kernel(peers, groups, tokens_ref, dq_ref, grad_kv_ref, w_ref, early_ref, earlies_ref, lates_ref, parts_ref, sums_ref, grads, normed, part, late, sums, stats, sems, row_sems, own_sems):
    me, group = lax.axis_index("space"), lax.axis_index("head")
    signal_all(peers, groups)
    rows, width = tokens_ref.shape
    cols = dq_ref.shape[1]
    share = width // groups
    tiles, heads = grad_kv_ref.shape[:2]
    span = rows // tiles
    step = 256

    @pl.loop(0, rows // step)
    def _(i):
        at = pl.ds(pl.multiple_of(i * step, step), step)
        standard, mean, inverse = norm_rows(tokens_ref[at, :])
        normed[at, :] = standard.astype(BF16)
        stats[0, at, :] = jnp.broadcast_to(mean, (step, 128))
        stats[1, at, :] = jnp.broadcast_to(inverse, (step, 128))
        grads[at, :cols] = dq_ref[at, :]

    for t in range(tiles):
        pairs = [grad_kv_ref[t, h].T for h in range(heads)]
        at = slice(t * span, (t + 1) * span)
        grads[at, cols : 2 * cols] = jnp.concatenate([p[:, :HEAD_DIM] for p in pairs], 1)
        grads[at, 2 * cols :] = jnp.concatenate([p[:, HEAD_DIM:] for p in pairs], 1)

    def chunk(k):
        at_cols = pl.ds(pl.multiple_of(lax.rem(group + k, groups) * share, share), share)

        @pl.loop(0, rows // step)
        def _(i):
            at = pl.ds(pl.multiple_of(i * step, step), step)
            piece = dot(grads[at, :cols], w_ref[0, at_cols, :], ((1,), (1,)))
            for n in (1, 2):
                lanes = slice(n * cols, (n + 1) * cols)
                piece += dot(grads[at, lanes], w_ref[n, at_cols, :], ((1,), (1,)))
            part[k, at, :] = piece.astype(BF16)
            values = tokens_ref[at, at_cols].astype(F32)
            standard = (values - stats[0, at, :1]) * stats[1, at, :1]
            found = [
                jnp.sum(piece, 1, keepdims=True),
                jnp.sum(piece * standard, 1, keepdims=True),
            ]
            found = jnp.concatenate(found, 1).T
            if k == 2:
                sums[:, at] = found
            else:
                sums[:, at] += found

    def across(k):
        return copy_to(
            part.at[k], parts_ref.at[group], row_sems, k, {"head": lax.rem(group + k, groups)}
        )

    def across_sums(k):
        return copy_to(
            sums, sums_ref.at[group], row_sems, groups + k, {"head": lax.rem(group + k, groups)}
        )

    def along(kind, r, peer):
        source, target = ((early_ref, earlies_ref), (late, lates_ref))[kind]
        return copy_to(
            source.at[peer], target.at[me], sems, kind * peers + r, {"space": peer}
        )

    owns = [
        pltpu.make_async_copy(early_ref.at[me], earlies_ref.at[me], own_sems.at[0]),
        pltpu.make_async_copy(late.at[me], lates_ref.at[me], own_sems.at[1]),
        pltpu.make_async_copy(part.at[0], parts_ref.at[group], own_sems.at[2]),
        pltpu.make_async_copy(sums, sums_ref.at[group], own_sems.at[3]),
    ]
    owns[0].start()
    pl.semaphore_wait(pltpu.get_barrier_semaphore(), peers + groups - 2)
    each_peer(lambda r, torus: along(0, r, torus_peer(me, torus)).start())
    chunk(2)
    across(2).start()
    piece = width // 4
    for i in range(4):
        made = dot(normed[:, i * piece : (i + 1) * piece], grads[...], ((0,), (0,)))
        late[i * peers // 4 : (i + 1) * peers // 4] = made.astype(BF16).reshape(
            peers // 4, width // peers, 3 * cols
        )
    owns[1].start()
    each_peer(lambda r, torus: along(1, r, torus_peer(me, torus)).start())
    for k in (1, 3):
        chunk(k)
        across(k).start()
    chunk(0)
    owns[2].start()
    owns[3].start()
    for k in range(1, groups):
        across_sums(k).start()

    @pl.loop(0, (peers - 1))
    def _(r):
        along(0, r, lax.rem(me + 1, peers)).wait()
        along(1, r, lax.rem(me + 1, peers)).wait()

    for k in range(1, groups):
        across(k).wait()
        across_sums(k).wait()
    for own in owns:
        own.wait()


def finish(tokens, dq, grad_kv, w3, early, peers, groups, number):
    rows, width = tokens.shape
    cols = dq.shape[1]
    whole = pl.BlockSpec(memory_space=pl.ANY)
    vmem = pl.BlockSpec(memory_space=pltpu.VMEM)
    part = (groups, rows, width // groups)
    late = (peers, width // peers, 3 * cols)
    return pl.pallas_call(
        functools.partial(finish_kernel, peers, groups),
        in_specs=[vmem] * 4 + [whole],
        out_specs=[whole] * 4,
        out_shape=[
            jax.ShapeDtypeStruct(early.shape, BF16),
            jax.ShapeDtypeStruct(late, BF16),
            jax.ShapeDtypeStruct(part, BF16),
            jax.ShapeDtypeStruct((groups, 2, rows), F32),
        ],
        scratch_shapes=[
            pltpu.VMEM((rows, 3 * cols), BF16),
            pltpu.VMEM((rows, width), BF16),
            pltpu.VMEM(part, BF16),
            pltpu.VMEM(late, BF16),
            pltpu.VMEM((2, rows), F32),
            pltpu.VMEM((2, rows, 128), F32),
            pltpu.SemaphoreType.DMA((2, 2 * peers)),
            pltpu.SemaphoreType.DMA((2, 2 * groups)),
            pltpu.SemaphoreType.DMA((4,)),
        ],
        compiler_params=pltpu.CompilerParams(
            collective_id=number, has_side_effects=True, vmem_limit_bytes=VMEM_BYTES
        ),
    )(tokens, dq, grad_kv, w3, early)


def on_device(tokens, w_qkv, w_out, neighbours, requests, cotangent):
    row_count, width = tokens.shape
    tiles = neighbours.shape[0]
    rows = row_count // tiles
    cols = w_qkv.shape[2]
    peers, groups = lax.axis_size("space"), lax.axis_size("head")
    share = cotangent.shape[1]
    me = lax.axis_index("space")
    column = lax.axis_index("head") * share
    w3 = jnp.transpose(w_qkv, (1, 0, 2))

    normed, q, kv, stats, table = project(
        tokens, w3, requests[0].T, rows, peers, groups, 2 * len(REACHES) + 3
    )
    wanted = lax.dynamic_index_in_dim(table, me, 2, keepdims=False).T.reshape(-1)
    apart = jnp.abs(jnp.arange(peers)[:, None] - jnp.arange(peers)[None, :])
    apart = jnp.minimum(apart, peers - apart)
    reach = jnp.max(jnp.where(jnp.any(table[:, 1:] >= 0, axis=1), apart, 0))
    level = sum((reach > r).astype(jnp.int32) for r in REACHES)
    reaches = (*REACHES, peers)

    entries = neighbours.reshape(-1)
    count = entries.shape[0]
    place = jnp.arange(count, dtype=jnp.int32)
    lower = entries[None, :] < entries[:, None]
    lower |= (entries[None, :] == entries[:, None]) & (place[None, :] < place[:, None])
    rank = jnp.sum(lower.astype(jnp.int32), 1)
    ranked = (rank[None, :] == place[:, None]).astype(jnp.int32)
    perm = jnp.sum(ranked * place[None, :], 1)
    keys = jnp.arange(tiles + peers * SLOTS, dtype=jnp.int32)
    below = (entries[None, :] < keys[:, None]).astype(jnp.int32)
    last = jnp.sum((entries[None, :] <= keys[:, None]).astype(jnp.int32), 1) - 1
    starts = jnp.sum(below, 1)
    same = 1 - jnp.max((starts[None, :] == place[:, None]).astype(jnp.int32), 1)
    grad_kv, dq, early, attended = lax.switch(
        level,
        [
            functools.partial(core, peers=peers, groups=groups, reach=r, number=n)
            for n, r in enumerate(reaches)
        ],
        *(wanted, entries, perm, same, last, q, kv, w_out, cotangent),
    )
    early = early.reshape(peers, width // peers, cols)
    early, late, part, sums = finish(
        tokens, dq, grad_kv, w3, early, peers, groups, 2 * len(reaches)
    )

    own_tokens = lax.dynamic_slice_in_dim(tokens, column, share, 1).astype(F32)
    layer_out = (own_tokens + jnp.sum(attended.astype(F32), 0)).astype(BF16)
    mean, inverse = stats[0][:, None], stats[1][:, None]
    own_standard = (own_tokens - mean) * inverse
    own_part = jnp.sum(part.astype(F32), 0)
    means = (jnp.sum(sums, 0) / width)[:, :, None]
    grad_tokens = (
        cotangent.astype(F32) + inverse * (own_part - means[0] - own_standard * means[1])
    ).astype(BF16)
    grad_w_out = jnp.sum(early.astype(F32), 0).T
    grad_w_qkv = jnp.sum(late.astype(F32), 0).reshape(-1, 3, cols)
    return (layer_out, grad_tokens, grad_w_qkv, grad_w_out)


def solution(mesh):
    placed = (
        P("space", None),
        P(None, None, "head"),
        P("head", None),
        P("space", None),
        P("space", None, None),
        P("space", "head"),
    )
    return jax.shard_map(
        on_device,
        mesh=mesh,
        in_specs=placed,
        out_specs=(
            P("space", "head"),
            P("space", "head"),
            P("space", None, "head"),
            P("head", "space"),
        ),
        check_vma=False,
    )
```

profile of v0, /device:TPU:1, one launch (start us, length us, event | category | flops | bytes accessed | tf_op | source)
XLA Modules:
  0.0 179.1 jit_solution(4776098354459971684)
XLA Ops:
  0.6 0.0 copy-start
  0.6 0.8 reshape.39
  1.5 0.1 convert_reduce_fusion.4
  1.6 0.1 fusion.11
  1.7 16.4 %shard_map.93 = (bf16[1024,1024]{1,0:T(8,128)(2,1)}, bf16[1024,256]{1,0:T(8,128)(2,1)}, bf16[8,4,128,128]{3,2,1,0:T(8,128)(2,1)S(1)}, f32[2,1024]{1,0:T(2,128)}, s32[32,2,32]{2,1,0:T(2,128)}) custom-call(bf16[1024,1024]{1,0:T(8,128)(2,1)} %tokens_ref.3, bf16[3,1024,256]{2,1,0:T(8,128)(2,1)} %bitcast.19, s32[2,32]{1,0:T(2,128)} %bitcast.31), custom_call_target="tpu_custom_call" | custom-call | tf_op jit(solution)/shard_map/pallas_call | solution.py:87
  18.1 0.8 fusion.14
  18.9 0.8 slice_compare_fusion
  19.6 0.6 fusion.13
  20.9 0.9 constant_dynamic-slice_fusion
  21.8 0.1 copy.11
  21.9 0.0 copy-done
  21.9 110.3 %conditional.1 = ((bf16[8,4,128,128]{3,2,1,0:T(8,128)(2,1)}, bf16[1024,256]{1,0:T(8,128)(2,1)}, bf16[1024,256]{1,0:T(8,128)(2,1)}, bf16[4,1024,256]{2,1,0:T(8,128)(2,1)})) conditional(s32[]{:T(128)} %clamp.3, (s32[2,32]{1,0:T(2,128)S(1)}, s32[72,72]{1,0:T(8,128)S(1)}, s32[72,72]{1,0:T(8,128)S(1)}, s32[72,72]{1,0:T(8,128)S(1)}, ...), branch_computations={%region_2.7_spmd, %region_7.12_spmd} | conditional | flops 30960 | bytes 106804 | solution.py:650
  21.9 0.6 reshape.34.wanted_ref
  22.5 0.1 reduce_sum.101
  22.6 0.6 select_reduce_fusion.perm_ref
  23.2 0.1 reduce_sum.103
  23.4 0.1 reduce_max.24
  23.5 0.5 broadcast_add_fusion
  24.0 107.8 %branch_0_fun.2 = (bf16[8,4,128,128]{3,2,1,0:T(8,128)(2,1)}, bf16[1024,256]{1,0:T(8,128)(2,1)}, bf16[1024,256]{1,0:T(8,128)(2,1)}, bf16[4,1024,256]{2,1,0:T(8,128)(2,1)}) custom-call(s32[64]{0:T(128)} %reshape.34.wanted_ref, s32[72]{0:T(128)S(1)} %get-tuple-element.162.entries_ref, s32[72]{0:T(128)} %select_reduce_fusion.perm_ref, ...), custom_call_target="tpu_custom_call" | custom-call | tf_op jit(solution)/shard_map/cond/branch_0_fun/pallas_call | solution.py:446
  132.2 0.0 copy-start.2
  132.2 0.0 copy-start.4
  132.2 0.0 copy-start.5
  132.2 2.1 %convert_reduce_fusion = f32[1024,256]{1,0:T(8,128)S(1)} fusion(bf16[4,1024,256]{2,1,0:T(8,128)(2,1)} %get-tuple-element.226), kind=kLoop, calls=%fused_computation.6 | loop fusion | flops 1835008 | bytes 3145728 | tf_op jit(solution)/shard_map/reduce_sum | solution.py:664
  134.4 0.0 copy-done.2
  134.4 0.0 copy-done.4
  134.4 0.0 copy-done.5
  134.4 38.4 %shard_map.94 = (bf16[32,32,256]{2,1,0:T(8,128)(2,1)}, bf16[32,32,768]{2,1,0:T(8,128)(2,1)}, bf16[4,1024,256]{2,1,0:T(8,128)(2,1)}, f32[4,2,1024]{2,1,0:T(2,128)}) custom-call(bf16[1024,1024]{1,0:T(8,128)(2,1)} %tokens_ref.3, bf16[1024,256]{1,0:T(8,128)(2,1)S(1)} %copy-done.4, bf16[8,4,128,128]{3,2,1,0:T(8,128)(2,1)S(1)} %copy-done.2, ...), custom_call_target="tpu_custom_call" | custom-call | tf_op jit(solution)/shard_map/pallas_call | solution.py:589
  172.7 0.0 copy-start.6
  172.8 2.0 %convert_reduce_fusion.1 = f32[1024,256]{1,0:T(8,128)S(1)} fusion(bf16[4,1024,256]{2,1,0:T(8,128)(2,1)} %get-tuple-element.207), kind=kLoop, calls=%fused_computation.7 | loop fusion | flops 1835008 | bytes 3145728 | tf_op jit(solution)/shard_map/reduce_sum | solution.py:667
  174.7 0.0 copy-done.6
  174.8 0.0 copy-start.3
  174.8 0.0 copy-start.1
  174.8 2.7 %fusion.6 = (bf16[1024,256]{1,0:T(8,128)(2,1)}, bf16[1024,256]{1,0:T(8,128)(2,1)}) fusion(f32[1024,256]{1,0:T(8,128)S(1)} %convert_reduce_fusion.1, bf16[1024,256]{1,0:T(8,128)(2,1)S(1)} %copy-done, f32[1024]{0:T(1024)S(1)} %bitcast.28, f32[1024]{0:T(1024)S(1)} %bitcast.26, f32[1024]{0:T(1024)S(1)} %bitcast.27, f32[1024]{0:T(1024)S(1)} %bitcast.25, ...), kind=kLoop, calls=%fused_computation.17 | loop fusion | flops 3145728 | bytes 4210692 | tf_op jit(solution)/shard_map/convert_element_type | solution.py:671
  177.6 0.0 copy-done.3
  177.6 0.7 convert_reduce_fusion.3
  178.3 0.0 copy-done.1
  178.3 0.2 convert_reduce_fusion.2
  178.5 0.6 copy.17
  (5 shorter events, 0.0 us)
Async XLA Ops:
  0.6 21.3 %copy-start = (bf16[1024,256]{1,0:T(8,128)(2,1)S(1)}, bf16[1024,256]{1,0:T(8,128)(2,1)}, u32[]{:S(2)}) copy-start(bf16[1024,256]{1,0:T(8,128)(2,1)} %param.13) | copy-start | bytes 1572868
  132.2 2.2 %copy-start.2 = (bf16[8,4,128,128]{3,2,1,0:T(8,128)(2,1)S(1)}, bf16[8,4,128,128]{3,2,1,0:T(8,128)(2,1)}, u32[]{:S(2)}) copy-start(bf16[8,4,128,128]{3,2,1,0:T(8,128)(2,1)} %get-tuple-element.229.grad_kv_ref) | copy-start | bytes 3145732
  132.2 2.2 %copy-start.4 = (bf16[1024,256]{1,0:T(8,128)(2,1)S(1)}, bf16[1024,256]{1,0:T(8,128)(2,1)}, u32[]{:S(2)}) copy-start(bf16[1024,256]{1,0:T(8,128)(2,1)} %get-tuple-element.228.dq_ref) | copy-start | bytes 1572868
  132.2 2.2 %copy-start.5 = (bf16[1024,256]{1,0:T(8,128)(2,1)S(1)}, bf16[1024,256]{1,0:T(8,128)(2,1)}, u32[]{:S(2)}) copy-start(bf16[1024,256]{1,0:T(8,128)(2,1)} %get-tuple-element.227) | copy-start | bytes 1572868
  172.7 2.0 %copy-start.6 = (f32[4,2,1024]{2,1,0:T(2,128)S(1)}, f32[4,2,1024]{2,1,0:T(2,128)}, u32[]{:S(2)}) copy-start(f32[4,2,1024]{2,1,0:T(2,128)} %get-tuple-element.208) | copy-start | bytes 98308
  174.8 2.7 %copy-start.3 = (bf16[32,32,256]{2,1,0:T(8,128)(2,1)S(1)}, bf16[32,32,256]{2,1,0:T(8,128)(2,1)}, u32[]{:S(2)}) copy-start(bf16[32,32,256]{2,1,0:T(8,128)(2,1)} %get-tuple-element.210) | copy-start | bytes 1572868
  174.8 3.4 %copy-start.1 = (bf16[32,32,768]{2,1,0:T(8,128)(2,1)S(1)}, bf16[32,32,768]{2,1,0:T(8,128)(2,1)}, u32[]{:S(2)}) copy-start(bf16[32,32,768]{2,1,0:T(8,128)(2,1)} %get-tuple-element.209) | copy-start | bytes 4718596
where the time goes:
time: 180 us; the launch traced here: 179 us
  Pallas kernels  163 us (91%)
  other arithmetic  10.9 us (6%)
  local copies, waits for them, and re-layouts  3.85 us (2%)
    pallas_call x1, Pallas kernels, core(): pl.pallas_call(functools.partial(core_kernel, peers, groups, reach), in_s...  108 us
    pallas_call x1, Pallas kernels, finish(): pl.pallas_call(functools.partial(finish_kernel, peers, groups), in_specs=...  38.4 us
    pallas_call x1, Pallas kernels, project(): pl.pallas_call(functools.partial(project_kernel, peers, groups), grid=(ro...  16.4 us

commit v1 on v0

--- a/solution.py
+++ b/solution.py
@@ -36,7 +36,7 @@
     return slice(h * HEAD_DIM, (h + 1) * HEAD_DIM)
 
 
-def project_kernel(peers, groups, tokens_ref, w_ref, requests_ref, normed_ref, q_ref, kv_ref, stats_ref, table_ref, sems, own_sem):
+def project_kernel(peers, groups, tokens_ref, w_ref, requests_ref, q_ref, kv_ref, stats_ref, wanted_out_ref, reach_ref, table_ref, sems, own_sem):
     me = lax.axis_index("space")
     step = pl.program_id(0)
     heads = kv_ref.shape[1]
@@ -52,7 +52,6 @@
 
     standard, mean, inverse = norm_rows(tokens_ref[...])
     normed = standard.astype(BF16)
-    normed_ref[...] = normed
     stats_ref[...] = jnp.concatenate([mean, inverse], 1).T
     q = dot(normed, w_ref[0], ((1,), (0,))).astype(BF16)
     q_ref[...] = (q.astype(F32) * HEAD_DIM ** (-0.5)).astype(BF16)
@@ -77,6 +76,18 @@
             along(r, lax.rem(me + r, peers)).wait()
 
         own.wait()
+        source = lax.broadcasted_iota(jnp.int32, (peers, peers), 0)
+        target = lax.broadcasted_iota(jnp.int32, (peers, peers), 1)
+        found = []
+        for c in range(SLOTS):
+            asked = table_ref[:, c, :].astype(F32)
+            found.append(jnp.sum(jnp.where(target == me, asked, 0.0), 1, keepdims=True))
+        wanted_out_ref[...] = jnp.concatenate(found, 1).astype(jnp.int32)
+        apart = jnp.abs(source - target)
+        apart = jnp.minimum(apart, peers - apart).astype(F32)
+        apart = jnp.where(table_ref[:, 1, :] >= 0, apart, 0.0)
+        apart = jnp.max(jnp.max(apart, 1, keepdims=True), 0, keepdims=True)
+        reach_ref[...] = apart.astype(jnp.int32)
 
 
 def project(tokens, w3, requests, tile_rows, peers, groups, number):
@@ -93,20 +104,24 @@
             pl.BlockSpec(memory_space=pl.ANY),
         ],
         out_specs=[
-            pl.BlockSpec((step, width), lambda i: (i, 0)),
             pl.BlockSpec((step, cols), lambda i: (i, 0)),
             pl.BlockSpec(kv_block, lambda i: (i, 0, 0, 0)),
             pl.BlockSpec((2, step), lambda i: (0, i)),
-            pl.BlockSpec(memory_space=pl.ANY),
+            pl.BlockSpec((peers, SLOTS), lambda i: (0, 0)),
+            pl.BlockSpec((1, 1), lambda i: (0, 0)),
         ],
         out_shape=[
-            jax.ShapeDtypeStruct((rows, width), BF16),
             jax.ShapeDtypeStruct((rows, cols), BF16),
             jax.ShapeDtypeStruct((rows // tile_rows,) + kv_block[1:], BF16),
             jax.ShapeDtypeStruct((2, rows), F32),
-            jax.ShapeDtypeStruct((peers,) + requests.shape, requests.dtype),
-        ],
-        scratch_shapes=[pltpu.SemaphoreType.DMA((2, peers)), pltpu.SemaphoreType.DMA],
+            jax.ShapeDtypeStruct((peers, SLOTS), requests.dtype),
+            jax.ShapeDtypeStruct((1, 1), requests.dtype),
+        ],
+        scratch_shapes=[
+            pltpu.VMEM((peers,) + requests.shape, requests.dtype),
+            pltpu.SemaphoreType.DMA((2, peers)),
+            pltpu.SemaphoreType.DMA,
+        ],
         compiler_params=pltpu.CompilerParams(
             collective_id=number, has_side_effects=True, vmem_limit_bytes=VMEM_BYTES
         ),
@@ -256,7 +271,7 @@
         @each_peer
         def _(i, step, half=half, cut=cut):
             peer = torus_peer(me, step)
-            staged[half][i] = kv_ref[jnp.maximum(wanted_ref[peer], 0), cut]
+            staged[half][i] = kv_ref[jnp.maximum(wanted_ref[peer, 0], 0), cut]
             send(half, 0, i, peer).start()
 
         for low, high in second_ranges(peers, reach):
@@ -264,7 +279,7 @@
             @pl.loop(low, high)
             def _(r, half=half, cut=cut):
                 peer = lax.rem(me + r, peers)
-                tile = jnp.maximum(wanted_ref[peers + peer], 0)
+                tile = jnp.maximum(wanted_ref[peer, 1], 0)
                 staged[half][peers + r] = kv_ref[tile, cut]
                 send(half, 1, r, peer).start()
 
@@ -408,7 +423,7 @@
     for half in range(2):
 
         def add(c, r, source, half=half):
-            tile = wanted_ref[c * peers + source]
+            tile = wanted_ref[source, c]
             block = landed[half][c * peers + r].astype(F32)
 
             @pl.loop(0, tiles)
@@ -613,6 +628,10 @@
     )(tokens, dq, grad_kv, w3, early)
 
 
+def add_up(pieces):
+    return sum(pieces[i].astype(F32) for i in range(pieces.shape[0]))
+
+
 def on_device(tokens, w_qkv, w_out, neighbours, requests, cotangent):
     row_count, width = tokens.shape
     tiles = neighbours.shape[0]
@@ -620,18 +639,13 @@
     cols = w_qkv.shape[2]
     peers, groups = lax.axis_size("space"), lax.axis_size("head")
     share = cotangent.shape[1]
-    me = lax.axis_index("space")
     column = lax.axis_index("head") * share
     w3 = jnp.transpose(w_qkv, (1, 0, 2))
 
-    normed, q, kv, stats, table = project(
+    q, kv, stats, wanted, reach = project(
         tokens, w3, requests[0].T, rows, peers, groups, 2 * len(REACHES) + 3
     )
-    wanted = lax.dynamic_index_in_dim(table, me, 2, keepdims=False).T.reshape(-1)
-    apart = jnp.abs(jnp.arange(peers)[:, None] - jnp.arange(peers)[None, :])
-    apart = jnp.minimum(apart, peers - apart)
-    reach = jnp.max(jnp.where(jnp.any(table[:, 1:] >= 0, axis=1), apart, 0))
-    level = sum((reach > r).astype(jnp.int32) for r in REACHES)
+    level = sum((reach[0, 0] > r).astype(jnp.int32) for r in REACHES)
     reaches = (*REACHES, peers)
 
     entries = neighbours.reshape(-1)
@@ -661,11 +675,11 @@
     )
 
     own_tokens = lax.dynamic_slice_in_dim(tokens, column, share, 1).astype(F32)
-    layer_out = (own_tokens + jnp.sum(attended.astype(F32), 0)).astype(BF16)
+    layer_out = (own_tokens + add_up(attended)).astype(BF16)
     mean, inverse = stats[0][:, None], stats[1][:, None]
     own_standard = (own_tokens - mean) * inverse
-    own_part = jnp.sum(part.astype(F32), 0)
-    means = (jnp.sum(sums, 0) / width)[:, :, None]
+    own_part = add_up(part)
+    means = (add_up(sums) / width)[:, :, None]
     grad_tokens = (
         cotangent.astype(F32) + inverse * (own_part - means[0] - own_standard * means[1])
     ).astype(BF16)

time: 180 us -> 173 us (0.961)
  other arithmetic: 10.9 us -> 6.56 us
  local copies, waits for them, and re-layouts: 3.85 us -> 1.68 us
    reduce_sum x3 -> x0, other arithmetic: 4.13 us -> none  [the longest x1 2.12 us: on_device(): layer_out = (own_tokens + jnp.sum(attended.astype(F32), 0)).astype(BF16)]
    pallas_call x1, Pallas kernels: 108 us -> 110 us  [core(): pl.pallas_call(functools.partial(core_kernel, peers, groups, reach), in_s...]
    pallas_call x1, Pallas kernels: 38.4 us -> 36.5 us  [finish(): pl.pallas_call(functools.partial(finish_kernel, peers, groups), in_specs=...]
where the time goes in v1:
time: 173 us
  Pallas kernels  163 us (94%)
  other arithmetic  6.56 us (4%)
    pallas_call x1, Pallas kernels, core(): pl.pallas_call(functools.partial(core_kernel, peers, groups, reach), in_s...  110 us
    pallas_call x1, Pallas kernels, finish(): pl.pallas_call(functools.partial(finish_kernel, peers, groups), in_specs=...  36.5 us
    pallas_call x1, Pallas kernels, project(): pl.pallas_call(functools.partial(project_kernel, peers, groups), grid=(ro...  16.2 us

profile of v1, /device:TPU:1, one launch (start us, length us, event | category | flops | bytes accessed | tf_op | source)
XLA Modules:
  0.0 172.7 jit_solution(6699443259589558065)
XLA Ops:
  0.6 0.0 copy-start
  0.6 0.8 reshape.58
  1.5 0.1 convert_reduce_fusion.2
  1.6 0.1 fusion.11
  1.7 16.2 %shard_map.93 = (bf16[1024,256]{1,0:T(8,128)(2,1)}, bf16[8,4,128,128]{3,2,1,0:T(8,128)(2,1)S(1)}, f32[2,1024]{1,0:T(2,128)}, s32[32,2]{1,0:T(8,128)S(1)}, s32[1,1]{1,0:T(1,128)}) custom-call(bf16[1024,1024]{1,0:T(8,128)(2,1)} %tokens_ref.3, bf16[3,1024,256]{2,1,0:T(8,128)(2,1)} %bitcast.21, s32[2,32]{1,0:T(2,128)} %bitcast.31), custom_call_target="tpu_custom_call" | custom-call | tf_op jit(solution)/shard_map/pallas_call | solution.py:98
  18.4 0.0 copy-done
  18.4 112.0 %conditional.1 = ((bf16[8,4,128,128]{3,2,1,0:T(8,128)(2,1)}, bf16[1024,256]{1,0:T(8,128)(2,1)}, bf16[1024,256]{1,0:T(8,128)(2,1)}, bf16[4,1024,256]{2,1,0:T(8,128)(2,1)})) conditional(s32[]{:T(128)} %bitcast.3, (s32[72,72]{1,0:T(8,128)S(1)}, s32[72,72]{1,0:T(8,128)S(1)}, s32[72,72]{1,0:T(8,128)S(1)}, s32[72,72]{1,0:T(8,128)S(1)}, ...), branch_computations={%region_1.6_spmd, %region_6.11_spmd} | conditional | flops 30960 | bytes 106292 | solution.py:664
  18.4 0.1 reduce_max.16
  18.6 0.1 reduce_sum.74
  18.7 0.5 broadcast_add_fusion
  19.2 0.1 reduce_sum.72
  19.3 0.6 select_reduce_fusion.perm_ref
  19.9 110.1 %branch_0_fun.2 = (bf16[8,4,128,128]{3,2,1,0:T(8,128)(2,1)}, bf16[1024,256]{1,0:T(8,128)(2,1)}, bf16[1024,256]{1,0:T(8,128)(2,1)}, bf16[4,1024,256]{2,1,0:T(8,128)(2,1)}) custom-call(s32[32,2]{1,0:T(8,128)S(1)} %get-tuple-element.152.wanted_ref, s32[72]{0:T(128)S(1)} %get-tuple-element.153.entries_ref, s32[72]{0:T(128)} %select_reduce_fusion.perm_ref, ...), custom_call_target="tpu_custom_call" | custom-call | tf_op jit(solution)/shard_map/cond/branch_0_fun/pallas_call | solution.py:461
  130.5 0.0 copy-start.4
  130.5 0.0 copy-start.1
  130.5 36.5 %shard_map.94 = (bf16[32,32,256]{2,1,0:T(8,128)(2,1)}, bf16[32,32,768]{2,1,0:T(8,128)(2,1)}, bf16[4,1024,256]{2,1,0:T(8,128)(2,1)}, f32[4,2,1024]{2,1,0:T(2,128)}) custom-call(bf16[1024,1024]{1,0:T(8,128)(2,1)} %tokens_ref.3, bf16[1024,256]{1,0:T(8,128)(2,1)} %get-tuple-element.220.dq_ref, bf16[8,4,128,128]{3,2,1,0:T(8,128)(2,1)} %get-tuple-element.221.grad_kv_ref, ...), custom_call_target="tpu_custom_call" | custom-call | tf_op jit(solution)/shard_map/pallas_call | solution.py:604
  166.9 0.8 add_multiply_fusion
  167.7 0.0 copy-done.4
  167.7 0.0 copy-done.1
  167.8 0.0 copy-start.2
  167.8 3.2 %fusion.6 = (bf16[1024,256]{1,0:T(8,128)(2,1)}, bf16[1024,256]{1,0:T(8,128)(2,1)}) fusion(bf16[1024,256]{1,0:T(8,128)(2,1)S(1)} %copy-done, f32[1024]{0:T(1024)S(1)} %bitcast.28, f32[1024]{0:T(1024)S(1)} %bitcast.30, f32[1024]{0:T(1024)S(1)} %bitcast.27, bf16[4,1024,256]{2,1,0:T(8,128)(2,1)} %get-tuple-element.200, f32[1024]{0:T(1024)S(1)} %bitcast.29, ...), kind=kLoop, calls=%fused_computation.15 | loop fusion | flops 6815744 | bytes 6307844 | tf_op jit(solution)/shard_map/convert_element_type | solution.py:685
  171.0 0.0 copy-start.3
  171.0 0.0 copy-done.2
  171.0 0.2 convert_reduce_fusion
  171.2 0.6 copy.13
  171.8 0.2 copy-done.3
  172.0 0.7 convert_reduce_fusion.1
  (4 shorter events, 0.0 us)
Async XLA Ops:
  0.6 17.8 %copy-start = (bf16[1024,256]{1,0:T(8,128)(2,1)S(1)}, bf16[1024,256]{1,0:T(8,128)(2,1)}, u32[]{:S(2)}) copy-start(bf16[1024,256]{1,0:T(8,128)(2,1)} %param.13) | copy-start | bytes 1572868
  130.5 37.3 %copy-start.4 = (f32[2,1024]{1,0:T(2,128)S(1)}, f32[2,1024]{1,0:T(2,128)}, u32[]{:S(2)}) copy-start(f32[2,1024]{1,0:T(2,128)} %get-tuple-element.196) | copy-start | bytes 24580
  130.5 37.3 %copy-start.1 = (bf16[4,1024,256]{2,1,0:T(8,128)(2,1)S(1)}, bf16[4,1024,256]{2,1,0:T(8,128)(2,1)}, u32[]{:S(2)}) copy-start(bf16[4,1024,256]{2,1,0:T(8,128)(2,1)} %get-tuple-element.219) | copy-start | bytes 6291460
  167.8 3.2 %copy-start.2 = (bf16[32,32,768]{2,1,0:T(8,128)(2,1)S(1)}, bf16[32,32,768]{2,1,0:T(8,128)(2,1)}, u32[]{:S(2)}) copy-start(bf16[32,32,768]{2,1,0:T(8,128)(2,1)} %get-tuple-element.202) | copy-start | bytes 4718596
  171.0 1.0 copy-start.3

commit v2 on v1

--- a/solution.py
+++ b/solution.py
@@ -11,7 +11,7 @@
 NEIGHBOURS = 9
 NEAR = 4
 REACHES = (1,)
-AT_ONCE = 2
+AT_ONCE = 1
 CORE_VMEM = 62 * 2**20
 SLOTS = 2
 EPSILON = 1e-05

time: 173 us -> 173 us (level)
  no operation moved by 1% of the time
where the time goes in v2:
time: 173 us
  Pallas kernels  163 us (94%)
  other arithmetic  6.56 us (4%)
    pallas_call x1, Pallas kernels, core(): pl.pallas_call(functools.partial(core_kernel, peers, groups, reach), in_s...  110 us
    pallas_call x1, Pallas kernels, finish(): pl.pallas_call(functools.partial(finish_kernel, peers, groups), in_specs=...  36.5 us
    pallas_call x1, Pallas kernels, project(): pl.pallas_call(functools.partial(project_kernel, peers, groups), grid=(ro...  16.2 us

profile of v2, /device:TPU:1, one launch (start us, length us, event | category | flops | bytes accessed | tf_op | source)
XLA Modules:
  0.0 172.9 jit_solution(15891516087063560511)
XLA Ops:
  0.6 0.0 copy-start
  0.6 0.8 reshape.58
  1.5 0.1 convert_reduce_fusion.2
  1.6 0.1 fusion.11
  1.7 16.2 %shard_map.93 = (bf16[1024,256]{1,0:T(8,128)(2,1)}, bf16[8,4,128,128]{3,2,1,0:T(8,128)(2,1)S(1)}, f32[2,1024]{1,0:T(2,128)}, s32[32,2]{1,0:T(8,128)S(1)}, s32[1,1]{1,0:T(1,128)}) custom-call(bf16[1024,1024]{1,0:T(8,128)(2,1)} %tokens_ref.3, bf16[3,1024,256]{2,1,0:T(8,128)(2,1)} %bitcast.21, s32[2,32]{1,0:T(2,128)} %bitcast.31), custom_call_target="tpu_custom_call" | custom-call | tf_op jit(solution)/shard_map/pallas_call | solution.py:98
  18.4 0.0 copy-done
  18.4 112.1 %conditional.1 = ((bf16[8,4,128,128]{3,2,1,0:T(8,128)(2,1)}, bf16[1024,256]{1,0:T(8,128)(2,1)}, bf16[1024,256]{1,0:T(8,128)(2,1)}, bf16[4,1024,256]{2,1,0:T(8,128)(2,1)})) conditional(s32[]{:T(128)} %bitcast.3, (s32[72,72]{1,0:T(8,128)S(1)}, s32[72,72]{1,0:T(8,128)S(1)}, s32[72,72]{1,0:T(8,128)S(1)}, s32[72,72]{1,0:T(8,128)S(1)}, ...), branch_computations={%region_1.6_spmd, %region_6.11_spmd} | conditional | flops 30960 | bytes 106292 | solution.py:664
  18.4 0.1 reduce_max.16
  18.6 0.1 reduce_sum.74
  18.7 0.5 broadcast_add_fusion
  19.2 0.1 reduce_sum.72
  19.3 0.6 select_reduce_fusion.perm_ref
  19.9 110.2 %branch_0_fun.2 = (bf16[8,4,128,128]{3,2,1,0:T(8,128)(2,1)}, bf16[1024,256]{1,0:T(8,128)(2,1)}, bf16[1024,256]{1,0:T(8,128)(2,1)}, bf16[4,1024,256]{2,1,0:T(8,128)(2,1)}) custom-call(s32[32,2]{1,0:T(8,128)S(1)} %get-tuple-element.152.wanted_ref, s32[72]{0:T(128)S(1)} %get-tuple-element.153.entries_ref, s32[72]{0:T(128)} %select_reduce_fusion.perm_ref, ...), custom_call_target="tpu_custom_call" | custom-call | tf_op jit(solution)/shard_map/cond/branch_0_fun/pallas_call | solution.py:461
  130.5 0.0 copy-start.4
  130.6 0.0 copy-start.1
  130.6 36.5 %shard_map.94 = (bf16[32,32,256]{2,1,0:T(8,128)(2,1)}, bf16[32,32,768]{2,1,0:T(8,128)(2,1)}, bf16[4,1024,256]{2,1,0:T(8,128)(2,1)}, f32[4,2,1024]{2,1,0:T(2,128)}) custom-call(bf16[1024,1024]{1,0:T(8,128)(2,1)} %tokens_ref.3, bf16[1024,256]{1,0:T(8,128)(2,1)} %get-tuple-element.220.dq_ref, bf16[8,4,128,128]{3,2,1,0:T(8,128)(2,1)} %get-tuple-element.221.grad_kv_ref, ...), custom_call_target="tpu_custom_call" | custom-call | tf_op jit(solution)/shard_map/pallas_call | solution.py:604
  167.1 0.8 add_multiply_fusion
  167.9 0.0 copy-done.4
  167.9 0.0 copy-done.1
  167.9 0.0 copy-start.2
  167.9 3.2 %fusion.6 = (bf16[1024,256]{1,0:T(8,128)(2,1)}, bf16[1024,256]{1,0:T(8,128)(2,1)}) fusion(bf16[1024,256]{1,0:T(8,128)(2,1)S(1)} %copy-done, f32[1024]{0:T(1024)S(1)} %bitcast.28, f32[1024]{0:T(1024)S(1)} %bitcast.30, f32[1024]{0:T(1024)S(1)} %bitcast.27, bf16[4,1024,256]{2,1,0:T(8,128)(2,1)} %get-tuple-element.200, f32[1024]{0:T(1024)S(1)} %bitcast.29, ...), kind=kLoop, calls=%fused_computation.15 | loop fusion | flops 6815744 | bytes 6307844 | tf_op jit(solution)/shard_map/convert_element_type | solution.py:685
  171.1 0.0 copy-start.3
  171.1 0.0 copy-done.2
  171.1 0.2 convert_reduce_fusion
  171.4 0.6 copy.13
  172.0 0.2 copy-done.3
  172.2 0.7 convert_reduce_fusion.1
  (4 shorter events, 0.0 us)
Async XLA Ops:
  0.6 17.8 %copy-start = (bf16[1024,256]{1,0:T(8,128)(2,1)S(1)}, bf16[1024,256]{1,0:T(8,128)(2,1)}, u32[]{:S(2)}) copy-start(bf16[1024,256]{1,0:T(8,128)(2,1)} %param.13) | copy-start | bytes 1572868
  130.5 37.3 %copy-start.4 = (f32[2,1024]{1,0:T(2,128)S(1)}, f32[2,1024]{1,0:T(2,128)}, u32[]{:S(2)}) copy-start(f32[2,1024]{1,0:T(2,128)} %get-tuple-element.196) | copy-start | bytes 24580
  130.6 37.4 %copy-start.1 = (bf16[4,1024,256]{2,1,0:T(8,128)(2,1)S(1)}, bf16[4,1024,256]{2,1,0:T(8,128)(2,1)}, u32[]{:S(2)}) copy-start(bf16[4,1024,256]{2,1,0:T(8,128)(2,1)} %get-tuple-element.219) | copy-start | bytes 6291460
  167.9 3.2 %copy-start.2 = (bf16[32,32,768]{2,1,0:T(8,128)(2,1)S(1)}, bf16[32,32,768]{2,1,0:T(8,128)(2,1)}, u32[]{:S(2)}) copy-start(bf16[32,32,768]{2,1,0:T(8,128)(2,1)} %get-tuple-element.202) | copy-start | bytes 4718596
  171.1 1.0 copy-start.3
